TPU v7x, 256 devices: a whole 4x4x8 slice. The times are simulated.
256 devices in a mesh: row: 16 (over z, core), col: 8 (over y_hi, x), rep: 2 (over y_lo).
Axes of the slice: x: 4, y: 4 (y_hi: 2, y_lo: 2; y = y_hi * 2 + y_lo), z: 8, core: 2. Of those that a mesh axis runs over, the one named last changes fastest.
Arguments:
- node_features: bfloat16 [65536, 256], P(('row', 'col', 'rep')), may hold values from -6 to 6
- weight: bfloat16 [256, 256], replicated, may hold values from -0.375 to 0.375
- cotangent: bfloat16 [65536, 256], P(('col', 'rep', 'row')), may hold values from -6 to 6
- adjacency_blocks: bfloat16 [16, 16, 256, 128, 128], P(('col', 'rep'), 'row'), may hold values from -0.0625 to 0.0625
- block_coords: int32 [16, 16, 2, 256], P(('col', 'rep'), 'row'), may hold values from 0 to 31, as said below
- block_counts: int32 [16, 16], P(('col', 'rep'), 'row'), may hold values from 1 to 256, as said below
Outputs:
- hidden: bfloat16 [65536, 256], P(('col', 'rep', 'row'))
- weight_grad: float32 [256, 256], replicated
- feature_grad: bfloat16 [65536, 256], P(('row', 'col', 'rep'))
Inputs may be any that keep to these rules, and one draw needn't show every extreme that they name: block_coords[i, r, 0, k] is a block row below 32 and block_coords[i, r, 1, k] a block column below 32; within a tile the first min(256, 1024) slots name distinct positions. Only the first block_counts[i, r] slots of tile (i, r) belong to the adjacency; the values and coordinates in its other slots are not part of it.
All inputs are finite; a program needn't handle non-finite values.
Results may differ from a plain program's by a relative error of at most 0.029.
Values may be sent and summed in bfloat16 or wider, within the bound.
No kernel may reach another device: no remote copies, remote signals or barrier semaphores. Data moves between devices by JAX's collectives and lax.ppermute only.
A program may use at most 128 MiB of HBM per device.

v0:
```python
import math
import jax
import jax.numpy as jnp
from jax import lax
from jax.sharding import PartitionSpec as P


def silu_slope(values):
    sigma = jax.nn.sigmoid(values)
    return sigma * (1.0 + values * (1.0 - sigma))


def tile_product(blocks, coords, filled, source, out_blocks, flipped):
    slot_total = blocks.shape[0]
    block_size = blocks.shape[1]
    feature_width = source.shape[1]
    group_size = math.gcd(slot_total, 64)
    groups = slot_total // group_size
    source_blocks = source.reshape(-1, block_size, feature_width)
    take_index = coords[0] if flipped else coords[1]
    put_index = coords[1] if flipped else coords[0]
    active = (jnp.arange(slot_total, dtype=jnp.int32) < filled).astype(jnp.float32)
    einsum_form = "kba,kbf->kaf" if flipped else "kab,kbf->kaf"
    targets = jnp.arange(out_blocks, dtype=jnp.int32)

    def accumulate(running, pieces):
        block_group, take_group, put_group, active_group = pieces
        gathered = source_blocks[take_group]
        product = jnp.einsum(einsum_form, block_group, gathered, preferred_element_type=jnp.float32)
        placing = (put_group[:, None] == targets[None, :]).astype(jnp.float32) * active_group[
            :, None
        ]
        flat = product.reshape(group_size, block_size * feature_width)
        placed = lax.dot_general(
            placing,
            flat,
            (((0,), (0,)), ((), ())),
            precision=lax.Precision.HIGHEST,
            preferred_element_type=jnp.float32,
        )
        return (running + placed, None)

    running = jnp.zeros((out_blocks, block_size * feature_width), jnp.float32)
    running, _ = lax.scan(
        accumulate,
        running,
        (
            blocks.reshape(groups, group_size, block_size, block_size),
            take_index.reshape(groups, group_size),
            put_index.reshape(groups, group_size),
            active.reshape(groups, group_size),
        ),
    )
    return running.reshape(out_blocks * block_size, feature_width)


def body(node_features, weight, cotangent, adjacency_blocks, block_coords, block_counts):
    blocks = adjacency_blocks[0, 0]
    coords = block_coords[0, 0]
    filled = block_counts[0, 0]
    block_size = blocks.shape[-1]
    local_nodes = node_features.shape[0]
    row_devices = lax.axis_size("row")
    node_total = local_nodes * row_devices * lax.axis_size("col") * lax.axis_size("rep")
    tile_rows = local_nodes * row_devices
    column_feats = lax.all_gather(node_features, ("col", "rep"), axis=0, tiled=True)
    tile_cols = column_feats.shape[0]
    partial_value = tile_product(
        blocks, coords, filled, column_feats, tile_rows // block_size, False
    )
    own_sum = lax.psum_scatter(
        partial_value.astype(jnp.bfloat16), "row", scatter_dimension=0, tiled=True
    )
    pre_act = jnp.dot(own_sum, weight, preferred_element_type=jnp.float32)
    hidden = jax.nn.silu(pre_act).astype(jnp.bfloat16)
    own_grad = (cotangent.astype(jnp.float32) * silu_slope(pre_act)).astype(jnp.bfloat16)
    own_mixed_grad = jnp.dot(own_grad, weight.T, preferred_element_type=jnp.float32).astype(
        jnp.bfloat16
    )
    panel_grad = lax.all_gather(own_mixed_grad, "row", axis=0, tiled=True)
    weight_part = lax.dot_general(
        own_sum, own_grad, (((0,), (0,)), ((), ())), preferred_element_type=jnp.float32
    )
    weight_grad = lax.psum(weight_part, ("row", "col", "rep")) / math.sqrt(node_total)
    back_terms = tile_product(blocks, coords, filled, panel_grad, tile_cols // block_size, True)
    feature_grad = lax.psum_scatter(
        back_terms.astype(jnp.bfloat16), ("col", "rep"), scatter_dimension=0, tiled=True
    )
    return (hidden, weight_grad, feature_grad)


def solution(mesh):
    in_specs = (
        P(("row", "col", "rep"), None),
        P(),
        P(("col", "rep", "row"), None),
        P(("col", "rep"), "row", None, None, None),
        P(("col", "rep"), "row", None, None),
        P(("col", "rep"), "row"),
    )
    out_specs = (P(("col", "rep", "row"), None), P(), P(("row", "col", "rep"), None))
    return jax.shard_map(body, mesh=mesh, in_specs=in_specs, out_specs=out_specs, check_vma=False)
```

profile of v0, /device:TPU:32, one launch (start us, length us, event | category | flops | bytes accessed | tf_op | source)
XLA Modules:
  0.0 642.4 jit_solution(17018396184696318942)
XLA Ops:
  9.6 81.7 %all-gather.3.cloned.1.call-done = bf16[4096,256]{1,0:T(8,128)(2,1)} async-done(((bf16[256,256]{1,0:T(8,128)(2,1)}), bf16[4096,256]{1,0:T(8,128)(2,1)}) %all-gather.3.cloned.1.call-update) | async-done | bytes 2097168 | tf_op jit(solution)/shard_map/all_gather | solution.py:66
  91.3 99.7 %while.22 = (s32[]{:T(128)}, f32[32,32768]{1,0:T(8,128)}, s32[4,64]{1,0:T(4,128)S(1)}, f32[4,64]{1,0:T(4,128)S(1)}, bf16[4,64,128,128]{3,2,1,0:T(8,128)(2,1)}, /...) while((s32[]{:T(128)}, f32[32,32768]{1,0:T(8,128)}, ...), condition=%wide.region_1.2_spmd.clone, body=%wide.region_0.1_spmd.clone.sunk | while | flops 1344279808 | bytes 56630384 | solution.py:44
  91.3 4.3 gather_fusion
  95.7 4.1 fusion.63
  99.7 8.0 %copy.16 = f32[8,8,128,256]{3,1,2,0:T(8,128)} copy(f32[8,8,128,256]{3,2,1,0:T(8,128)S(1)} %bitcast.88) | data formatting | bytes 16777216 | tf_op jit(solution)/shard_map/while
  107.7 8.0 %convolution_add_fusion.4 = f32[32,32768]{1,0:T(8,128)} fusion(f32[64,32768]{1,0:T(8,128)} %bitcast.86, f32[32,32768]{1,0:T(8,128)} %get-tuple-element.276, pred[]{:T(512)S(6)} %compare.6, f32[64]{0:T(128)S(1)} %fusion.64, s32[64]{0:T(128)S(1)} %fusion.65), kind=kOutput, calls=%fused_computation.4.clone.1 | convolution fusion | flops 807407616 | bytes 16777728 | tf_op jit(solution)/shard_map/while/body/eval_jaxpr/dot_general | solution.py:34
  115.7 4.3 gather_fusion
  120.1 4.1 fusion.63
  124.1 8.0 %copy.16 = f32[8,8,128,256]{3,1,2,0:T(8,128)} copy(f32[8,8,128,256]{3,2,1,0:T(8,128)S(1)} %bitcast.88) | data formatting | bytes 16777216 | tf_op jit(solution)/shard_map/while
  132.1 8.7 %convolution_add_fusion.4 = f32[32,32768]{1,0:T(8,128)} fusion(f32[64,32768]{1,0:T(8,128)} %bitcast.86, f32[32,32768]{1,0:T(8,128)} %get-tuple-element.276, pred[]{:T(512)S(6)} %compare.6, f32[64]{0:T(128)S(1)} %fusion.64, s32[64]{0:T(128)S(1)} %fusion.65), kind=kOutput, calls=%fused_computation.4.clone.1 | convolution fusion | flops 807407616 | bytes 16777728 | tf_op jit(solution)/shard_map/while/body/eval_jaxpr/dot_general | solution.py:34
  140.8 4.3 gather_fusion
  145.2 4.1 fusion.63
  149.2 8.0 %copy.16 = f32[8,8,128,256]{3,1,2,0:T(8,128)} copy(f32[8,8,128,256]{3,2,1,0:T(8,128)S(1)} %bitcast.88) | data formatting | bytes 16777216 | tf_op jit(solution)/shard_map/while
  157.2 8.7 %convolution_add_fusion.4 = f32[32,32768]{1,0:T(8,128)} fusion(f32[64,32768]{1,0:T(8,128)} %bitcast.86, f32[32,32768]{1,0:T(8,128)} %get-tuple-element.276, pred[]{:T(512)S(6)} %compare.6, f32[64]{0:T(128)S(1)} %fusion.64, s32[64]{0:T(128)S(1)} %fusion.65), kind=kOutput, calls=%fused_computation.4.clone.1 | convolution fusion | flops 807407616 | bytes 16777728 | tf_op jit(solution)/shard_map/while/body/eval_jaxpr/dot_general | solution.py:34
  165.9 4.3 gather_fusion
  170.2 4.1 fusion.63
  174.3 8.0 %copy.16 = f32[8,8,128,256]{3,1,2,0:T(8,128)} copy(f32[8,8,128,256]{3,2,1,0:T(8,128)S(1)} %bitcast.88) | data formatting | bytes 16777216 | tf_op jit(solution)/shard_map/while
  182.3 8.7 %convolution_add_fusion.4 = f32[32,32768]{1,0:T(8,128)} fusion(f32[64,32768]{1,0:T(8,128)} %bitcast.86, f32[32,32768]{1,0:T(8,128)} %get-tuple-element.276, pred[]{:T(512)S(6)} %compare.6, f32[64]{0:T(128)S(1)} %fusion.64, s32[64]{0:T(128)S(1)} %fusion.65), kind=kOutput, calls=%fused_computation.4.clone.1 | convolution fusion | flops 807407616 | bytes 16777728 | tf_op jit(solution)/shard_map/while/body/eval_jaxpr/dot_general | solution.py:34
  191.0 2.4 convert_element_type.32
  193.4 2.4 convert_element_type.33
  195.8 56.5 %reduce-scatter.3.cloned.1.call-done = bf16[256,256]{1,0:T(8,128)(2,1)} async-done(((bf16[4096,256]{1,0:T(8,128)(2,1)}), bf16[256,256]{1,0:T(8,128)(2,1)}) %reduce-scatter.3.cloned.1.call-update) | async-done | bytes 131088 | tf_op jit(solution)/shard_map/reduce_scatter | solution.py:71
  252.3 1.8 multiply_convert_fusion
  254.1 0.9 convolution_convert_fusion
  255.1 12.0 %copy.9 = bf16[1,1,256,128,128]{3,4,2,1,0:T(8,128)(2,1)} copy(bf16[1,1,256,128,128]{4,3,2,1,0:T(8,128)(2,1)} %bitcast.93) | data formatting | bytes 16777216 | tf_op args[3]
  267.1 0.9 fusion.31
  268.3 27.7 %all-gather.5.cloned.1.call-done = bf16[4096,256]{1,0:T(8,128)(2,1)} async-done(((bf16[256,256]{1,0:T(8,128)(2,1)}), bf16[4096,256]{1,0:T(8,128)(2,1)}) %all-gather.5.cloned.1.call-update) | async-done | bytes 2097168 | tf_op jit(solution)/shard_map/all_gather | solution.py:80
  296.0 99.8 %while.23 = (s32[]{:T(128)}, f32[32,32768]{1,0:T(8,128)}, s32[4,64]{1,0:T(4,128)S(1)}, f32[4,64]{1,0:T(4,128)S(1)}, bf16[4,64,128,128]{2,3,1,0:T(8,128)(2,1)}, /...) while((s32[]{:T(128)}, f32[32,32768]{1,0:T(8,128)}, ...), condition=%wide.region_5.6_spmd.clone, body=%wide.region_4.5_spmd.clone.sunk | while | flops 1344279808 | bytes 56630384 | solution.py:44
  296.0 4.4 gather_fusion.1
  300.4 4.1 fusion.71
  304.5 8.0 %copy.17 = f32[8,8,128,256]{3,1,2,0:T(8,128)} copy(f32[8,8,128,256]{3,2,1,0:T(8,128)S(1)} %bitcast.89) | data formatting | bytes 16777216 | tf_op jit(solution)/shard_map/while
  312.4 8.0 %convolution_add_fusion.5 = f32[32,32768]{1,0:T(8,128)} fusion(f32[64,32768]{1,0:T(8,128)} %bitcast.87, f32[32,32768]{1,0:T(8,128)} %get-tuple-element.303, pred[]{:T(512)S(6)} %compare.7, f32[64]{0:T(128)S(1)} %fusion.72, s32[64]{0:T(128)S(1)} %fusion.73), kind=kOutput, calls=%fused_computation.24.clone.1 | convolution fusion | flops 807407616 | bytes 16777728 | tf_op jit(solution)/shard_map/while/body/eval_jaxpr/dot_general | solution.py:34
  320.4 4.4 gather_fusion.1
  324.8 4.1 fusion.71
  328.9 8.0 %copy.17 = f32[8,8,128,256]{3,1,2,0:T(8,128)} copy(f32[8,8,128,256]{3,2,1,0:T(8,128)S(1)} %bitcast.89) | data formatting | bytes 16777216 | tf_op jit(solution)/shard_map/while
  336.9 8.7 %convolution_add_fusion.5 = f32[32,32768]{1,0:T(8,128)} fusion(f32[64,32768]{1,0:T(8,128)} %bitcast.87, f32[32,32768]{1,0:T(8,128)} %get-tuple-element.303, pred[]{:T(512)S(6)} %compare.7, f32[64]{0:T(128)S(1)} %fusion.72, s32[64]{0:T(128)S(1)} %fusion.73), kind=kOutput, calls=%fused_computation.24.clone.1 | convolution fusion | flops 807407616 | bytes 16777728 | tf_op jit(solution)/shard_map/while/body/eval_jaxpr/dot_general | solution.py:34
  345.6 4.4 gather_fusion.1
  350.0 4.1 fusion.71
  354.1 8.0 %copy.17 = f32[8,8,128,256]{3,1,2,0:T(8,128)} copy(f32[8,8,128,256]{3,2,1,0:T(8,128)S(1)} %bitcast.89) | data formatting | bytes 16777216 | tf_op jit(solution)/shard_map/while
  362.0 8.6 %convolution_add_fusion.5 = f32[32,32768]{1,0:T(8,128)} fusion(f32[64,32768]{1,0:T(8,128)} %bitcast.87, f32[32,32768]{1,0:T(8,128)} %get-tuple-element.303, pred[]{:T(512)S(6)} %compare.7, f32[64]{0:T(128)S(1)} %fusion.72, s32[64]{0:T(128)S(1)} %fusion.73), kind=kOutput, calls=%fused_computation.24.clone.1 | convolution fusion | flops 807407616 | bytes 16777728 | tf_op jit(solution)/shard_map/while/body/eval_jaxpr/dot_general | solution.py:34
  370.7 4.4 gather_fusion.1
  375.1 4.1 fusion.71
  379.2 8.0 %copy.17 = f32[8,8,128,256]{3,1,2,0:T(8,128)} copy(f32[8,8,128,256]{3,2,1,0:T(8,128)S(1)} %bitcast.89) | data formatting | bytes 16777216 | tf_op jit(solution)/shard_map/while
  387.1 8.7 %convolution_add_fusion.5 = f32[32,32768]{1,0:T(8,128)} fusion(f32[64,32768]{1,0:T(8,128)} %bitcast.87, f32[32,32768]{1,0:T(8,128)} %get-tuple-element.303, pred[]{:T(512)S(6)} %compare.7, f32[64]{0:T(128)S(1)} %fusion.72, s32[64]{0:T(128)S(1)} %fusion.73), kind=kOutput, calls=%fused_computation.24.clone.1 | convolution fusion | flops 807407616 | bytes 16777728 | tf_op jit(solution)/shard_map/while/body/eval_jaxpr/dot_general | solution.py:34
  395.8 2.4 convert_element_type.38
  398.2 2.4 convert_element_type.39
  400.6 148.2 %all-reduce.2.cloned.1.call-done = f32[256,256]{1,0:T(8,128)} async-done(((f32[256,256]{1,0:T(8,128)}), f32[256,256]{1,0:T(8,128)}) %all-reduce.2.cloned.1.call-update) | async-done | bytes 262160 | tf_op jit(solution)/shard_map/psum | solution.py:84
  548.9 1.7 broadcast_multiply_fusion
  550.5 85.3 %reduce-scatter.5.cloned.1.call-done = bf16[256,256]{1,0:T(8,128)(2,1)} async-done(((bf16[4096,256]{1,0:T(8,128)(2,1)}), bf16[256,256]{1,0:T(8,128)(2,1)}) %reduce-scatter.5.cloned.1.call-update) | async-done | bytes 131088 | tf_op jit(solution)/shard_map/reduce_scatter | solution.py:86
  (56 shorter events, 2.3 us)
Async XLA Ops:
  7.2 245.1 %copy-start = (bf16[256,256]{1,0:T(8,128)(2,1)S(1)}, bf16[256,256]{1,0:T(8,128)(2,1)}, u32[]{:S(2)}) copy-start(bf16[256,256]{1,0:T(8,128)(2,1)} %param.11) | copy-start | bytes 393220
  7.2 84.1 %all-gather.3.cloned.1.call-start = ((), (), s32[]{:S(2)}) async-start(), calls=%async_computation.2 | async-start | bytes 2228224 | tf_op jit(solution)/shard_map/all_gather | solution.py:66
  7.9 244.4 %reduce-scatter.3.cloned.1.call-start = ((), (), s32[]{:S(2)}) async-start(), calls=%async_computation.3 | async-start | bytes 2228224 | tf_op jit(solution)/shard_map/reduce_scatter | solution.py:71
  193.4 58.9 %copy-start.3 = (bf16[256,256]{1,0:T(8,128)(2,1)S(1)}, bf16[256,256]{1,0:T(8,128)(2,1)}, u32[]{:S(2)}) copy-start(bf16[256,256]{1,0:T(8,128)(2,1)} %param.12) | copy-start | bytes 393220
  195.8 100.3 %all-gather.5.cloned.1.call-start = ((), (), s32[]{:S(2)}) async-start(), calls=%async_computation.5 | async-start | bytes 2228224 | tf_op jit(solution)/shard_map/all_gather | solution.py:80
  255.0 12.1 %copy-start.2 = (bf16[256,256]{1,0:T(8,128)(2,1)S(1)}, bf16[256,256]{1,0:T(8,128)(2,1)}, u32[]{:S(2)}) copy-start(bf16[256,256]{1,0:T(8,128)(2,1)} %reduce-scatter.3.cloned.1.call-done) | copy-start | bytes 393220
  255.0 293.8 %all-reduce.2.cloned.1.call-start = ((), (), s32[]{:S(2)}) async-start(), calls=%async_computation.4 | async-start | bytes 524288 | tf_op jit(solution)/shard_map/psum | solution.py:84
  268.1 367.8 %reduce-scatter.5.cloned.1.call-start = ((), (), s32[]{:S(2)}) async-start(), calls=%async_computation.6 | async-start | bytes 2228224 | tf_op jit(solution)/shard_map/reduce_scatter | solution.py:86
  395.8 240.0 %copy-start.1 = (bf16[256,256]{1,0:T(8,128)(2,1)S(1)}, bf16[256,256]{1,0:T(8,128)(2,1)}, u32[]{:S(2)}) copy-start(bf16[256,256]{1,0:T(8,128)(2,1)} %param.11) | copy-start | bytes 393220
Sparse Core Ops, SparseCore 0:
  9.8 81.4 all-gather.2
  195.9 56.3 reduce-scatter.2
  255.2 40.8 all-gather.4
  301.9 246.9 all-reduce.1
  551.8 83.9 reduce-scatter.4
where the time goes:
time: 643 us; the launch traced here: 642 us
  waiting for transfers between devices  400 us (62%)
  local copies, waits for them, and re-layouts  116 us (18%)
  matrix products  104 us (16%)
  between operations  14.5 us (2%)
  other arithmetic  6.61 us (1%)
    psum x1, waiting for transfers between devices, body(): lax.psum(weight_part, ('row', 'col', 'rep')) / math.sqrt(node_total)  148 us
    reduce_scatter x1, waiting for transfers between devices, body(): lax.psum_scatter(back_terms.astype(jnp.bfloat16), ('col', 'rep'), scatter...  85.3 us
    all_gather x1, waiting for transfers between devices, body(): lax.all_gather(node_features, ('col', 'rep'), axis=0, tiled=True)  81.7 us
    dot_general x8, matrix products, accumulate(): lax.dot_general(placing, flat, (((0,), (0,)), ((), ())), precision=lax.Pr...  68 us
    while x8, local copies, waits for them, and re-layouts  63.7 us
    reduce_scatter x1, waiting for transfers between devices, body(): lax.psum_scatter(partial_value.astype(jnp.bfloat16), 'row', scatter_dimen...  56.5 us
    gather x8, local copies, waits for them, and re-layouts, accumulate(): gathered = source_blocks[take_group]  34.8 us
    dot_general x8, matrix products, accumulate(): jnp.einsum(einsum_form, block_group, gathered, preferred_element_type=jnp...  32.6 us
  transfers between devices with their start and end apart: 5, of which 5 were waited for; matrix products, arithmetic and copies ran while one was open for 19% of the time, Pallas kernels for 0%

commit v1 on v0

--- a/solution.py
+++ b/solution.py
@@ -77,7 +77,40 @@
     own_mixed_grad = jnp.dot(own_grad, weight.T, preferred_element_type=jnp.float32).astype(
         jnp.bfloat16
     )
-    panel_grad = lax.all_gather(own_mixed_grad, "row", axis=0, tiled=True)
+    known = lax.axis_size("row")
+    local_now = lax.axis_index("row")
+    mid_arr, kept_arr, opened = (known, local_now, own_mixed_grad.shape[0])
+    steps_seen = []
+    k = 0
+    while k < mid_arr:
+        steps_seen.append((k, (k + 1) % mid_arr))
+        k = k + 1
+    pool = []
+    k = 0
+    while k < mid_arr:
+        pool.append((k, (k - 1) % mid_arr))
+        k += 1
+    panel_grad = jnp.zeros(
+        (*own_mixed_grad.shape[:0], mid_arr * opened, *own_mixed_grad.shape[1:]),
+        own_mixed_grad.dtype,
+    )
+    panel_grad = lax.dynamic_update_slice_in_dim(
+        panel_grad, own_mixed_grad, kept_arr * opened, axis=0
+    )
+    u_next = spare = own_mixed_grad
+    block_next = mid_arr // 2
+    b = 1
+    while b < block_next + 1:
+        u_next = lax.ppermute(u_next, "row", steps_seen)
+        panel_grad = lax.dynamic_update_slice_in_dim(
+            panel_grad, u_next, (kept_arr - b) % mid_arr * opened, axis=0
+        )
+        if b < mid_arr - block_next:
+            spare = lax.ppermute(spare, perm=pool, axis_name="row")
+            panel_grad = lax.dynamic_update_slice_in_dim(
+                panel_grad, spare, (kept_arr + b) % mid_arr * opened, axis=0
+            )
+        b = b + 1
     weight_part = lax.dot_general(
         own_sum, own_grad, (((0,), (0,)), ((), ())), preferred_element_type=jnp.float32
     )

time: 643 us -> 603 us (0.938)
  waiting for transfers between devices: 400 us -> 349 us
  starting transfers between devices: 0.38 us -> 17.6 us
    psum x1, waiting for transfers between devices: 148 us -> 115 us  [body(): lax.psum(weight_part, ('row', 'col', 'rep')) / math.sqrt(node_total)]
    all_gather x1 -> x0, waiting for transfers between devices: 27.7 us -> none  [body(): panel_grad = lax.all_gather(own_mixed_grad, 'row', axis=0, tiled=True)]
    ppermute x0 -> x15, waiting for transfers between devices: none -> 22.2 us  [the longest x8 22.1 us: body(): u_next = lax.ppermute(u_next, 'row', steps_seen)]
    ppermute x0 -> x15, starting transfers between devices: none -> 17.3 us  [the longest x7 17.3 us: body(): spare = lax.ppermute(spare, perm=pool, axis_name='row')]
    reduce_scatter x1, waiting for transfers between devices: 56.5 us -> 44.3 us  [body(): lax.psum_scatter(partial_value.astype(jnp.bfloat16), 'row', scatter_dimen...]
  transfers between devices with their start and end apart: 5 -> 19, of which waited for: 5 -> 12; matrix products, arithmetic and copies ran while one was open for 19% -> 19% of each run, Pallas kernels for 0% -> 0%
where the time goes in v1:
time: 603 us; the launch traced here: 602 us
  waiting for transfers between devices  349 us (58%)
  local copies, waits for them, and re-layouts  110 us (18%)
  matrix products  104 us (17%)
  starting transfers between devices  17.6 us (3%)
  between operations  14.9 us (2%)
  other arithmetic  6.58 us (1%)
    psum x1, waiting for transfers between devices, body(): lax.psum(weight_part, ('row', 'col', 'rep')) / math.sqrt(node_total)  115 us
    reduce_scatter x1, waiting for transfers between devices, body(): lax.psum_scatter(back_terms.astype(jnp.bfloat16), ('col', 'rep'), scatter...  85.3 us
    all_gather x1, waiting for transfers between devices, body(): lax.all_gather(node_features, ('col', 'rep'), axis=0, tiled=True)  81.7 us
    dot_general x8, matrix products, accumulate(): lax.dot_general(placing, flat, (((0,), (0,)), ((), ())), precision=lax.Pr...  68.1 us
    while x8, local copies, waits for them, and re-layouts  63.8 us
    reduce_scatter x1, waiting for transfers between devices, body(): lax.psum_scatter(partial_value.astype(jnp.bfloat16), 'row', scatter_dimen...  44.3 us
    dot_general x8, matrix products, accumulate(): jnp.einsum(einsum_form, block_group, gathered, preferred_element_type=jnp...  32.5 us
    gather x8, local copies, waits for them, and re-layouts, accumulate(): gathered = source_blocks[take_group]  28.5 us
  transfers between devices with their start and end apart: 19, of which 12 were waited for; matrix products, arithmetic and copies ran while one was open for 19% of the time, Pallas kernels for 0%

profile of v1, /device:TPU:32, one launch (start us, length us, event | category | flops | bytes accessed | tf_op | source)
XLA Modules:
  0.0 602.3 jit_solution(9687051765063613450)
XLA Ops:
  9.6 81.7 %all-gather.2.cloned.1.call-done = bf16[4096,256]{1,0:T(8,128)(2,1)} async-done(((bf16[256,256]{1,0:T(8,128)(2,1)}), bf16[4096,256]{1,0:T(8,128)(2,1)}) %all-gather.2.cloned.1.call-update) | async-done | bytes 2097168 | tf_op jit(solution)/shard_map/all_gather | solution.py:66
  91.3 99.8 %while.22 = (s32[]{:T(128)}, f32[32,32768]{1,0:T(8,128)}, s32[4,64]{1,0:T(4,128)S(1)}, f32[4,64]{1,0:T(4,128)S(1)}, bf16[4,64,128,128]{3,2,1,0:T(8,128)(2,1)}, /...) while((s32[]{:T(128)}, f32[32,32768]{1,0:T(8,128)}, ...), condition=%wide.region_1.2_spmd.clone, body=%wide.region_0.1_spmd.clone.sunk | while | flops 1344279808 | bytes 56630384 | solution.py:44
  91.3 4.3 gather_fusion
  95.7 4.1 fusion.63
  99.7 8.0 %copy.16 = f32[8,8,128,256]{3,1,2,0:T(8,128)} copy(f32[8,8,128,256]{3,2,1,0:T(8,128)S(1)} %bitcast.88) | data formatting | bytes 16777216 | tf_op jit(solution)/shard_map/while
  107.7 8.0 %convolution_add_fusion.4 = f32[32,32768]{1,0:T(8,128)} fusion(f32[64,32768]{1,0:T(8,128)} %bitcast.86, f32[32,32768]{1,0:T(8,128)} %get-tuple-element.278, pred[]{:T(512)S(6)} %compare.21, f32[64]{0:T(128)S(1)} %fusion.64, s32[64]{0:T(128)S(1)} %fusion.65), kind=kOutput, calls=%fused_computation.4.clone.1 | convolution fusion | flops 807407616 | bytes 16777728 | tf_op jit(solution)/shard_map/while/body/eval_jaxpr/dot_general | solution.py:34
  115.8 4.3 gather_fusion
  120.1 4.1 fusion.63
  124.2 8.0 %copy.16 = f32[8,8,128,256]{3,1,2,0:T(8,128)} copy(f32[8,8,128,256]{3,2,1,0:T(8,128)S(1)} %bitcast.88) | data formatting | bytes 16777216 | tf_op jit(solution)/shard_map/while
  132.2 8.7 %convolution_add_fusion.4 = f32[32,32768]{1,0:T(8,128)} fusion(f32[64,32768]{1,0:T(8,128)} %bitcast.86, f32[32,32768]{1,0:T(8,128)} %get-tuple-element.278, pred[]{:T(512)S(6)} %compare.21, f32[64]{0:T(128)S(1)} %fusion.64, s32[64]{0:T(128)S(1)} %fusion.65), kind=kOutput, calls=%fused_computation.4.clone.1 | convolution fusion | flops 807407616 | bytes 16777728 | tf_op jit(solution)/shard_map/while/body/eval_jaxpr/dot_general | solution.py:34
  140.9 4.3 gather_fusion
  145.2 4.1 fusion.63
  149.3 8.0 %copy.16 = f32[8,8,128,256]{3,1,2,0:T(8,128)} copy(f32[8,8,128,256]{3,2,1,0:T(8,128)S(1)} %bitcast.88) | data formatting | bytes 16777216 | tf_op jit(solution)/shard_map/while
  157.3 8.7 %convolution_add_fusion.4 = f32[32,32768]{1,0:T(8,128)} fusion(f32[64,32768]{1,0:T(8,128)} %bitcast.86, f32[32,32768]{1,0:T(8,128)} %get-tuple-element.278, pred[]{:T(512)S(6)} %compare.21, f32[64]{0:T(128)S(1)} %fusion.64, s32[64]{0:T(128)S(1)} %fusion.65), kind=kOutput, calls=%fused_computation.4.clone.1 | convolution fusion | flops 807407616 | bytes 16777728 | tf_op jit(solution)/shard_map/while/body/eval_jaxpr/dot_general | solution.py:34
  166.0 4.3 gather_fusion
  170.3 4.1 fusion.63
  174.4 8.0 %copy.16 = f32[8,8,128,256]{3,1,2,0:T(8,128)} copy(f32[8,8,128,256]{3,2,1,0:T(8,128)S(1)} %bitcast.88) | data formatting | bytes 16777216 | tf_op jit(solution)/shard_map/while
  182.4 8.7 %convolution_add_fusion.4 = f32[32,32768]{1,0:T(8,128)} fusion(f32[64,32768]{1,0:T(8,128)} %bitcast.86, f32[32,32768]{1,0:T(8,128)} %get-tuple-element.278, pred[]{:T(512)S(6)} %compare.21, f32[64]{0:T(128)S(1)} %fusion.64, s32[64]{0:T(128)S(1)} %fusion.65), kind=kOutput, calls=%fused_computation.4.clone.1 | convolution fusion | flops 807407616 | bytes 16777728 | tf_op jit(solution)/shard_map/while/body/eval_jaxpr/dot_general | solution.py:34
  196.2 12.0 %copy.9 = bf16[1,1,256,128,128]{3,4,2,1,0:T(8,128)(2,1)} copy(bf16[1,1,256,128,128]{4,3,2,1,0:T(8,128)(2,1)} %bitcast.93) | data formatting | bytes 16777216 | tf_op args[3]
  208.2 44.3 %reduce-scatter.3.cloned.1.call-done = bf16[256,256]{1,0:T(8,128)(2,1)} async-done(((bf16[4096,256]{1,0:T(8,128)(2,1)}), bf16[256,256]{1,0:T(8,128)(2,1)}) %reduce-scatter.3.cloned.1.call-update) | async-done | bytes 131088 | tf_op jit(solution)/shard_map/reduce_scatter | solution.py:71
  261.1 2.6 collective-permute-done.2
  265.5 2.6 collective-permute-done.4
  268.1 2.8 collective-permute-start.7
  270.9 2.5 collective-permute-done.6
  273.4 3.1 collective-permute-start.9
  279.0 3.1 collective-permute-start.11
  282.1 2.5 collective-permute-done.10
  284.6 3.1 collective-permute-start.13
  290.3 5.6 collective-permute-done.14
  295.9 93.5 %while.23 = (s32[]{:T(128)}, f32[32,32768]{1,0:T(8,128)}, s32[4,64]{1,0:T(4,128)S(1)}, f32[4,64]{1,0:T(4,128)S(1)}, bf16[4,64,128,128]{2,3,1,0:T(8,128)(2,1)}, /...) while((s32[]{:T(128)}, f32[32,32768]{1,0:T(8,128)}, ...), condition=%wide.region_5.6_spmd.clone, body=%wide.region_4.5_spmd.clone.sunk | while | flops 1344279808 | bytes 56630384 | solution.py:44
  295.9 2.8 gather_fusion.1
  298.7 4.1 fusion.71
  302.8 8.0 %copy.17 = f32[8,8,128,256]{3,1,2,0:T(8,128)} copy(f32[8,8,128,256]{3,2,1,0:T(8,128)S(1)} %bitcast.89) | data formatting | bytes 16777216 | tf_op jit(solution)/shard_map/while
  310.7 8.0 %convolution_add_fusion.5 = f32[32,32768]{1,0:T(8,128)} fusion(f32[64,32768]{1,0:T(8,128)} %bitcast.87, f32[32,32768]{1,0:T(8,128)} %get-tuple-element.305, pred[]{:T(512)S(6)} %compare.22, f32[64]{0:T(128)S(1)} %fusion.72, s32[64]{0:T(128)S(1)} %fusion.73), kind=kOutput, calls=%fused_computation.24.clone.1 | convolution fusion | flops 807407616 | bytes 16777728 | tf_op jit(solution)/shard_map/while/body/eval_jaxpr/dot_general | solution.py:34
  318.8 2.8 gather_fusion.1
  321.6 4.1 fusion.71
  325.6 8.0 %copy.17 = f32[8,8,128,256]{3,1,2,0:T(8,128)} copy(f32[8,8,128,256]{3,2,1,0:T(8,128)S(1)} %bitcast.89) | data formatting | bytes 16777216 | tf_op jit(solution)/shard_map/while
  333.6 8.7 %convolution_add_fusion.5 = f32[32,32768]{1,0:T(8,128)} fusion(f32[64,32768]{1,0:T(8,128)} %bitcast.87, f32[32,32768]{1,0:T(8,128)} %get-tuple-element.305, pred[]{:T(512)S(6)} %compare.22, f32[64]{0:T(128)S(1)} %fusion.72, s32[64]{0:T(128)S(1)} %fusion.73), kind=kOutput, calls=%fused_computation.24.clone.1 | convolution fusion | flops 807407616 | bytes 16777728 | tf_op jit(solution)/shard_map/while/body/eval_jaxpr/dot_general | solution.py:34
  342.3 2.8 gather_fusion.1
  345.1 4.1 fusion.71
  349.2 8.0 %copy.17 = f32[8,8,128,256]{3,1,2,0:T(8,128)} copy(f32[8,8,128,256]{3,2,1,0:T(8,128)S(1)} %bitcast.89) | data formatting | bytes 16777216 | tf_op jit(solution)/shard_map/while
  357.2 8.7 %convolution_add_fusion.5 = f32[32,32768]{1,0:T(8,128)} fusion(f32[64,32768]{1,0:T(8,128)} %bitcast.87, f32[32,32768]{1,0:T(8,128)} %get-tuple-element.305, pred[]{:T(512)S(6)} %compare.22, f32[64]{0:T(128)S(1)} %fusion.72, s32[64]{0:T(128)S(1)} %fusion.73), kind=kOutput, calls=%fused_computation.24.clone.1 | convolution fusion | flops 807407616 | bytes 16777728 | tf_op jit(solution)/shard_map/while/body/eval_jaxpr/dot_general | solution.py:34
  365.9 2.8 gather_fusion.1
  368.6 4.1 fusion.71
  372.7 8.0 %copy.17 = f32[8,8,128,256]{3,1,2,0:T(8,128)} copy(f32[8,8,128,256]{3,2,1,0:T(8,128)S(1)} %bitcast.89) | data formatting | bytes 16777216 | tf_op jit(solution)/shard_map/while
  380.7 8.7 %convolution_add_fusion.5 = f32[32,32768]{1,0:T(8,128)} fusion(f32[64,32768]{1,0:T(8,128)} %bitcast.87, f32[32,32768]{1,0:T(8,128)} %get-tuple-element.305, pred[]{:T(512)S(6)} %compare.22, f32[64]{0:T(128)S(1)} %fusion.72, s32[64]{0:T(128)S(1)} %fusion.73), kind=kOutput, calls=%fused_computation.24.clone.1 | convolution fusion | flops 807407616 | bytes 16777728 | tf_op jit(solution)/shard_map/while/body/eval_jaxpr/dot_general | solution.py:34
  394.2 114.6 %all-reduce.2.cloned.1.call-done = f32[256,256]{1,0:T(8,128)} async-done(((f32[256,256]{1,0:T(8,128)}), f32[256,256]{1,0:T(8,128)}) %all-reduce.2.cloned.1.call-update) | async-done | bytes 262160 | tf_op jit(solution)/shard_map/psum | solution.py:117
  510.5 85.3 %reduce-scatter.5.cloned.1.call-done = bf16[256,256]{1,0:T(8,128)(2,1)} async-done(((bf16[4096,256]{1,0:T(8,128)(2,1)}), bf16[256,256]{1,0:T(8,128)(2,1)}) %reduce-scatter.5.cloned.1.call-update) | async-done | bytes 131088 | tf_op jit(solution)/shard_map/reduce_scatter | solution.py:119
  (99 shorter events, 28.6 us)
Async XLA Ops:
  7.2 245.4 %copy-start = (bf16[256,256]{1,0:T(8,128)(2,1)S(1)}, bf16[256,256]{1,0:T(8,128)(2,1)}, u32[]{:S(2)}) copy-start(bf16[256,256]{1,0:T(8,128)(2,1)} %param.11) | copy-start | bytes 393220
  7.2 84.1 %all-gather.2.cloned.1.call-start = ((), (), s32[]{:S(2)}) async-start(), calls=%async_computation.2 | async-start | bytes 2228224 | tf_op jit(solution)/shard_map/all_gather | solution.py:66
  7.9 244.7 %reduce-scatter.3.cloned.1.call-start = ((), (), s32[]{:S(2)}) async-start(), calls=%async_computation.3 | async-start | bytes 2228224 | tf_op jit(solution)/shard_map/reduce_scatter | solution.py:71
  195.9 312.9 %all-reduce.2.cloned.1.call-start = ((), (), s32[]{:S(2)}) async-start(), calls=%async_computation.4 | async-start | bytes 524288 | tf_op jit(solution)/shard_map/psum | solution.py:117
  196.2 56.4 %copy-start.3 = (bf16[256,256]{1,0:T(8,128)(2,1)S(1)}, bf16[256,256]{1,0:T(8,128)(2,1)}, u32[]{:S(2)}) copy-start(bf16[256,256]{1,0:T(8,128)(2,1)} %param.12) | copy-start | bytes 393220
  252.6 4.1 copy-start.2
  254.9 4.4 collective-permute-start
  254.9 4.4 collective-permute-start.1
  257.6 338.2 %reduce-scatter.5.cloned.1.call-start = ((), (), s32[]{:S(2)}) async-start(), calls=%async_computation.5 | async-start | bytes 2228224 | tf_op jit(solution)/shard_map/reduce_scatter | solution.py:119
  259.3 4.4 collective-permute-start.2
  259.3 4.4 collective-permute-start.3
  263.7 4.4 collective-permute-start.4
  263.7 4.4 collective-permute-start.5
  268.1 5.3 collective-permute-start.6
  268.1 5.3 collective-permute-start.7
  273.4 5.6 collective-permute-start.8
  273.4 5.6 collective-permute-start.9
  279.0 5.6 collective-permute-start.10
  279.0 5.6 collective-permute-start.11
  284.6 5.6 collective-permute-start.12
  284.6 5.6 collective-permute-start.13
  290.2 5.6 collective-permute-start.14
  391.8 204.0 %copy-start.1 = (bf16[256,256]{1,0:T(8,128)(2,1)S(1)}, bf16[256,256]{1,0:T(8,128)(2,1)}, u32[]{:S(2)}) copy-start(bf16[256,256]{1,0:T(8,128)(2,1)} %param.11) | copy-start | bytes 393220
Sparse Core Ops, SparseCore 0:
  9.8 81.4 all-gather.1
  196.0 56.5 reduce-scatter.2
  258.6 250.1 all-reduce.1
  511.8 83.9 reduce-scatter.4
